TPU v7x, 32 devices: a whole 2x2x4 slice. The times are simulated.
32 devices in a mesh: parts: 2 (over x), beam: 16 (over z, y, core).
Axes of the slice: x: 2, y: 2, z: 4, core: 2. Of those that a mesh axis runs over, the one named last changes fastest.
Arguments:
- smatrix: bfloat16 [144, 144, 4, 2048], P(None, None, 'parts', 'beam'), parts along dimension 2, may hold values from -6 to 6
- amplitude: float32 [2048], P('beam'), may hold values from 0.5 to 13.5
- aberration: float32 [2048], P('beam'), may hold values from -3.140625 to 3.140625
- beam_list: int32 [2048, 2], P('beam'), may hold values from -64 to 63
- positions: int32 [2, 64, 2], replicated, may hold values from 0 to 127
- anchors: int32 [2, 2], replicated, may hold values from 0 to 16
- masks: int32 [4, 128, 128], replicated, may hold values from 0 to 1, as said below
Outputs:
- signals: float32 [4, 64, 4], P('parts', 'beam'), parts along dimension 0
There are 2 independent parts, one for each index of `parts`. A program takes and returns all parts, laid end to end along the dimension named above; an argument that names none is the same for every part. Nothing has to cross between parts.
Inputs may be any that keep to these rules, and one draw needn't show every extreme that they name: `masks`: each detector's mask is 1 exactly on an annulus of wrapped frequency radii, every annulus holds some frequencies, and every masked frequency has wrapped radius squared below (63) squared.
All inputs are finite; a program needn't handle non-finite values.
Results may differ from a plain program's by a relative error of at most 0.00035.
Values sent between devices are 32-bit elements; how exact they have to be, the bound alone decides.
A program may use at most 128 MiB of HBM per device.

v0:
```python
import math

import jax
import jax.numpy as jnp
from jax import lax
from jax.sharding import PartitionSpec as P

TILES = 2


def coefficients(amplitude, aberration, beam_list, spots, width):
    phase_index = jnp.remainder(
        spots[:, 0:1] * beam_list[None, :, 0] + spots[:, 1:2] * beam_list[None, :, 1], width
    )
    theta = aberration[None, :] - 2.0 * math.pi / width * phase_index.astype(jnp.float32)
    coef_re = (amplitude[None, :] * jnp.cos(theta)).astype(jnp.bfloat16)
    coef_im = (amplitude[None, :] * jnp.sin(theta)).astype(jnp.bfloat16)
    upper = jnp.concatenate([coef_re, -coef_im], 1)
    lower = jnp.concatenate([coef_im, coef_re], 1)
    return jnp.stack([upper, lower], 1)


def window_of(smatrix, corner, width):
    zero = jnp.zeros((), jnp.int32)
    local_beams = smatrix.shape[3]
    window = lax.dynamic_slice(
        smatrix, (corner[0], corner[1], zero, zero), (width, width, 2, local_beams)
    )
    return window.reshape(width * width, 2 * local_beams)


def transform(wave_re, wave_im, width):
    freq = jnp.arange(width, dtype=jnp.int32)
    angle = (
        2.0
        * math.pi
        / width
        * jnp.remainder(freq[:, None] * freq[None, :], width).astype(jnp.float32)
    )
    cosine = jnp.cos(angle)
    sine = jnp.sin(angle)
    high = lax.Precision.HIGHEST
    half_re = jnp.einsum("nrs,sk->nrk", wave_re, cosine, precision=high) + jnp.einsum(
        "nrs,sk->nrk", wave_im, sine, precision=high
    )
    half_im = jnp.einsum("nrs,sk->nrk", wave_im, cosine, precision=high) - jnp.einsum(
        "nrs,sk->nrk", wave_re, sine, precision=high
    )
    full_re = jnp.einsum("jr,nrk->njk", cosine, half_re, precision=high) + jnp.einsum(
        "jr,nrk->njk", sine, half_im, precision=high
    )
    full_im = jnp.einsum("jr,nrk->njk", cosine, half_im, precision=high) - jnp.einsum(
        "jr,nrk->njk", sine, half_re, precision=high
    )
    return (full_re, full_im)


def wave_rows(left, right, count):
    rows = left
    rows = rows.reshape(2 * count, rows.shape[2])
    product = lax.dot_general(
        rows, right, (((1,), (1,)), ((), ())), preferred_element_type=jnp.float32
    )
    product = product.reshape(count, 2, right.shape[0])
    return product


def detect(owned, mask_table, norm, width):
    count = owned.shape[0]
    full_re, full_im = transform(
        owned[:, 0].reshape(count, width, width), owned[:, 1].reshape(count, width, width), width
    )
    power = (full_re * full_re + full_im * full_im).reshape(count, width * width)
    return jnp.einsum("np,dp->nd", power, mask_table, precision=lax.Precision.HIGHEST) / (
        norm * width * width
    )


def local(smatrix, amplitude, aberration, beam_list, positions, anchors, masks):
    width = masks.shape[1]
    detectors = masks.shape[0]
    pixels = width * width
    per_device = positions.shape[1] // lax.axis_size("beam")
    norm = lax.psum(jnp.sum(amplitude * amplitude), "beam")
    mask_table = masks.reshape(detectors, pixels).astype(jnp.float32)
    lefts = []
    rights = []
    for tile in range(TILES):
        lefts.append(coefficients(amplitude, aberration, beam_list, positions[tile], width))
        rights.append(window_of(smatrix, anchors[tile], width))
    outputs = []
    for tile in range(TILES):
        left = lefts[tile]
        right = rights[tile]
        owned = lax.psum_scatter(
            wave_rows(left, right, per_device * lax.axis_size("beam")),
            "beam",
            scatter_dimension=0,
            tiled=True,
        )
        outputs.append(detect(owned, mask_table, norm, width))
    return jnp.stack(outputs, 0)


def solution(mesh):
    placed = (P(None, None, "parts", "beam"), P("beam"), P("beam"), P("beam", None), P(), P(), P())
    return jax.shard_map(
        local, mesh=mesh, in_specs=placed, out_specs=P("parts", "beam", None), check_vma=False
    )
```

profile of v0, /device:TPU:0, one launch (start us, length us, event | category | flops | bytes accessed | tf_op | source)
XLA Modules:
  0.0 405.0 jit_solution(8796817262820651250)
XLA Ops:
  6.5 0.7 slice_bitcast_fusion.1
  7.2 0.8 slice_bitcast_fusion.6
  8.0 1.0 multiply_convert_fusion.2
  9.0 1.0 fusion.168
  10.1 1.4 fusion.170
  18.9 15.2 %constant_dynamic-slice_fusion.1 = (bf16[128,128,2,128]{3,2,1,0:T(2,128)(2,1)}, bf16[128,128,2,128]{3,2,1,0:T(2,128)(2,1)}) fusion(bf16[144,144,2,128]{3,2,1,0:T(2,128)(2,1)} %param.7, s32[]{:T(128)S(6)} %select_n.62, s32[]{:T(128)S(6)} %select_n.63, s32[]{:T(128)S(6)} %select_n.66, s32[]{:T(128)S(6)} %select_n.67), kind=kLoop, calls=%fused_computation.136 | loop fusion | bytes 33554448 | tf_op jit(solution)/shard_map/dynamic_slice | solution.py:26
  34.1 14.1 %reshape.33 = bf16[16384,256,1]{1,0,2:T(8,128)(2,1)} reshape(bf16[128,128,2,128]{3,2,1,0:T(2,128)(2,1)} %get-tuple-element.7) | data formatting | bytes 16777216 | tf_op jit(solution)/shard_map/reshape | solution.py:29
  48.2 14.1 %reshape.37 = bf16[16384,256,1]{1,0,2:T(8,128)(2,1)} reshape(bf16[128,128,2,128]{3,2,1,0:T(2,128)(2,1)} %get-tuple-element.8) | data formatting | bytes 16777216 | tf_op jit(solution)/shard_map/reshape | solution.py:29
  62.3 9.6 %fusion.41 = f32[64,2,16384]{2,0,1:T(8,128)} fusion(bf16[16384,256,1]{1,0,2:T(8,128)(2,1)} %reshape.33, bf16[64,1,256]{2,0,1:T(8,128)(2,1)S(1)} %get-tuple-element.14, bf16[64,1,256]{2,0,1:T(8,128)(2,1)S(1)} %get-tuple-element.13), kind=kOutput, calls=%fused_computation.54 | convolution fusion | flops 1073774592 | bytes 16842752 | tf_op jit(solution)/shard_map/dot_general | solution.py:61
  71.9 6.1 %fusion.45 = f32[64,2,16384]{2,0,1:T(8,128)} fusion(bf16[16384,256,1]{1,0,2:T(8,128)(2,1)S(1)} %copy-done, bf16[64,1,256]{2,0,1:T(8,128)(2,1)S(1)} %get-tuple-element.16, bf16[64,1,256]{2,0,1:T(8,128)(2,1)S(1)} %get-tuple-element.15), kind=kOutput, calls=%fused_computation.58 | convolution fusion | flops 1073774592 | bytes 16842752 | tf_op jit(solution)/shard_map/dot_general | solution.py:61
  78.0 0.6 copy-done.2
  79.2 37.3 %psum.7 = f32[]{:T(128)} all-reduce(f32[]{:T(128)} %multiply_reduce_fusion), channel_id=1, replica_groups=mesh['parts'=2,'beam'=16] {'beam'}, use_global_device_ids=true, to_apply=%region_2.3 | all-reduce | flops 1 | bytes 8 | tf_op jit(solution)/shard_map/psum | solution.py:84
  118.4 261.8 %all-reduce.5.cloned.1.call-done = (f32[64,2,16384]{2,0,1:T(8,128)}, f32[64,2,16384]{2,0,1:T(8,128)}) async-done(((f32[64,2,16384]{2,0,1:T(8,128)}, f32[64,2,16384]{2,0,1:T(8,128)}), (f32[64,2,16384]{2,0,1:T(8,128)}, f32[64,2,16384]{2,0,1:T(8,128)})) %all-reduce.5.cloned.1.call-update) | async-done | bytes 16777232
  380.1 1.3 dynamic-slice_bitcast_fusion.3
  381.4 0.6 fusion.14
  382.0 0.6 convolution_add_fusion.1
  382.7 0.7 fusion.70
  383.4 0.7 fusion.55
  384.1 0.6 fusion.10
  384.7 0.6 convolution_subtract_fusion.1
  385.4 0.7 fusion.57
  386.1 0.7 fusion.67
  386.8 1.3 dynamic-slice_bitcast_fusion.1
  388.7 0.6 convolution_add_fusion
  389.4 0.7 fusion.64
  390.1 0.7 fusion.49
  391.4 0.6 convolution_subtract_fusion
  392.1 0.7 fusion.51
  392.8 0.7 fusion.61
  394.8 1.4 fusion.1
  396.1 1.4 fusion.3
  397.5 0.6 pad_maximum_fusion
  (25 shorter events, 3.7 us)
Async XLA Ops:
  6.5 373.6 %all-reduce.5.cloned.1.call-start = ((), (), s32[]{:S(2)}) async-start(), calls=%async_computation | async-start | bytes 33554432
  62.3 9.6 %copy-start = (bf16[16384,256,1]{1,0,2:T(8,128)(2,1)S(1)}, bf16[16384,256,1]{1,0,2:T(8,128)(2,1)}, u32[]{:S(2)}) copy-start(bf16[16384,256,1]{1,0,2:T(8,128)(2,1)} %reshape.37) | copy-start | bytes 25165828
  78.0 0.7 copy-start.2
  78.0 38.5 %copy-start.1 = (s32[4,128,128]{2,1,0:T(8,128)S(1)}, s32[4,128,128]{2,1,0:T(8,128)}, u32[]{:S(2)}) copy-start(s32[4,128,128]{2,1,0:T(8,128)} %param.13) | copy-start | bytes 786436
  78.0 38.6 %copy-start.3 = (u32[32]{0:T(128)S(1)}, u32[32]{0:T(128)}, u32[]{:S(2)}) copy-start(u32[32]{0:T(128)} %constant.44) | copy-start | bytes 388
Sparse Core Ops, SparseCore 0:
  78.1 301.9 all-reduce.4
where the time goes:
time: 406 us; the launch traced here: 405 us
  waiting for transfers between devices  262 us (65%)
  local copies, waits for them, and re-layouts  51.3 us (13%)
  blocking collectives  37.3 us (9%)
  matrix products  29 us (7%)
  between operations  22.3 us (5%)
    unnamed x2, waiting for transfers between devices  262 us
    psum x1, blocking collectives, local(): norm = lax.psum(jnp.sum(amplitude * amplitude), 'beam')  37.3 us
    reshape x2, local copies, waits for them, and re-layouts, window_of(): return window.reshape(width * width, 2 * local_beams)  28.2 us
    dot_general x2, matrix products, wave_rows(): lax.dot_general(rows, right, (((1,), (1,)), ((), ())), preferred_element_...  15.6 us
    dynamic_slice x1, local copies, waits for them, and re-layouts, window_of(): lax.dynamic_slice(smatrix, (corner[0], corner[1], zero, zero), (width, wi...  15.2 us
  transfers between devices with their start and end apart: 1, of which 1 were waited for; matrix products, arithmetic and copies ran while one was open for 0% of the time, Pallas kernels for 0%

commit v1 on v0

--- a/solution.py
+++ b/solution.py
@@ -1,11 +1,18 @@
+import functools
 import math
 
 import jax
 import jax.numpy as jnp
+import numpy as np
 from jax import lax
+from jax.experimental import pallas as pl
+from jax.experimental.pallas import tpu as pltpu
 from jax.sharding import PartitionSpec as P
 
 TILES = 2
+ROUNDS = 8
+ROWS = 2
+MESH = pl.DeviceIdType.MESH
 
 
 def coefficients(amplitude, aberration, beam_list, spots, width):
@@ -102,8 +109,289 @@
     return jnp.stack(outputs, 0)
 
 
+def fourier(width):
+    index = np.arange(width)
+    angle = 2.0 * np.pi / width * (np.outer(index, index) % width)
+    return np.cos(angle), np.sin(angle)
+
+
+def halves(table):
+    high = table.astype(np.float32).astype(jnp.bfloat16)
+    low = (table - high.astype(np.float64)).astype(np.float32).astype(jnp.bfloat16)
+    return np.stack([high, low])
+
+
+def column_table(width):
+    cosine, sine = fourier(width)
+    table = np.zeros((width, 2, 2, width))
+    table[:, 0, 0] = cosine
+    table[:, 1, 0] = sine
+    table[:, 0, 1] = -sine
+    table[:, 1, 1] = cosine
+    return halves(table.reshape(2 * width, 2 * width))
+
+
+def reduce_kernel(
+    deep, width, anchors, matrix, coef, fold, power_in, table, out,
+    own, from_core, from_y, from_low, from_high,
+    send_c, recv_c, send_y, recv_y, send_r, recv_r, send_l, recv_l,
+):
+    me = lax.axis_index("beam")
+    core = lax.rem(me, 2)
+    side = lax.rem(me // 2, 2)
+    place = me // 4
+    other_core = me + 1 - 2 * core
+    other_side = me + 2 - 4 * side
+    above = me + 4
+    below = me - 4
+    first = place == 0
+    last = place == deep - 1
+
+    barrier = pltpu.get_barrier_semaphore()
+    for there in (other_core, other_side):
+        pl.semaphore_signal(barrier, inc=1, device_id={"beam": there}, device_id_type=MESH)
+
+    @pl.when(place > 0)
+    def _():
+        pl.semaphore_signal(barrier, inc=1, device_id={"beam": below}, device_id_type=MESH)
+
+    @pl.when(place < deep - 1)
+    def _():
+        pl.semaphore_signal(barrier, inc=1, device_id={"beam": above}, device_id_type=MESH)
+
+    pl.semaphore_wait(barrier, jnp.where(first | last, 3, 4))
+
+    chunk = width // ROUNDS
+    tail = fold.shape[2]
+    norm = jnp.sum(power_in[...] * power_in[...])
+    lane = lax.broadcasted_iota(jnp.int32, (coef.shape[0] // 2, width), 1)
+
+    def copy(source, target, send, recv, there):
+        return pltpu.make_async_remote_copy(
+            src_ref=source, dst_ref=target, send_sem=send, recv_sem=recv,
+            device_id={"beam": there}, device_id_type=MESH,
+        )
+
+    def core_copy(k):
+        return copy(own.at[k, 1 - core], from_core.at[k], send_c.at[k], recv_c.at[k], other_core)
+
+    def side_copy(k):
+        return copy(own.at[k, core, 1 - side], from_y.at[k], send_y.at[k], recv_y.at[k], other_side)
+
+    def up_copy(k, j):
+        return copy(
+            own.at[k, core, side, j], from_low.at[k, j], send_r.at[k, j], recv_r.at[k, j], above
+        )
+
+    def down_copy(k, j):
+        return copy(
+            own.at[k, core, side, j], from_high.at[k, j], send_l.at[k, j], recv_l.at[k, j], below
+        )
+
+    def window_row(i, tile):
+        row = i + jnp.where(i < anchors[tile, 0], width, 0)
+        values = matrix[row]
+        start = values[:tail] * fold[tile, 0] + values[2 * width :] * fold[tile, 1]
+        return jnp.concatenate([start, values[tail : 2 * width]], 0)
+
+    def compute(k):
+        def body(step, carry):
+            waves = []
+            for part in range(ROWS):
+                i = k * chunk + step * ROWS + part
+                right = jnp.concatenate([window_row(i, t) for t in range(TILES)], 1)
+                waves.append(
+                    lax.dot_general(
+                        coef[...], right, (((1,), (1,)), ((), ())),
+                        preferred_element_type=jnp.float32,
+                    )
+                )
+            wave = jnp.concatenate(waves, 0)
+            high = wave.astype(jnp.bfloat16)
+            low = (wave - high.astype(jnp.float32)).astype(jnp.bfloat16)
+            full = jnp.dot(high, table[0], preferred_element_type=jnp.float32)
+            full += jnp.dot(low, table[0], preferred_element_type=jnp.float32)
+            full += jnp.dot(high, table[1], preferred_element_type=jnp.float32)
+            count = coef.shape[0] // 2
+            shape = own.shape[1:4] + (8, width)
+            for part in range(ROWS):
+                a = full[2 * part * count : (2 * part + 1) * count]
+                b = full[(2 * part + 1) * count : (2 * part + 2) * count]
+                real = a[:, :width] - b[:, width:]
+                imag = a[:, width:] + b[:, :width]
+                real = jnp.where(lane == width // 2, norm, real)
+                own[k, :, :, :, step * ROWS + part, 0] = real.reshape(shape)
+                own[k, :, :, :, step * ROWS + part, 1] = imag.reshape(shape)
+            return carry
+
+        lax.fori_loop(0, chunk // ROWS, body, 0)
+
+    def phase(it, carry):
+        @pl.when(it < ROUNDS)
+        def _():
+            compute(it)
+            core_copy(it).start()
+
+        k1 = it - 1
+
+        @pl.when((k1 >= 0) & (k1 < ROUNDS))
+        def _():
+            core_copy(k1).wait_recv()
+            own[k1, core, 1 - side] += from_core[k1, 1 - side]
+            side_copy(k1).start()
+            own[k1, core, side] += from_core[k1, side]
+
+        k2 = it - 2
+
+        @pl.when((k2 >= 0) & (k2 < ROUNDS))
+        def _():
+            side_copy(k2).wait_recv()
+            own[k2, core, side] += from_y[k2]
+
+        ku = it - 2 - place
+
+        @pl.when((ku >= 0) & (ku < ROUNDS))
+        def _():
+            for j in range(deep - 1, 0, -1):
+
+                @pl.when(j > place)
+                def _():
+                    @pl.when(place > 0)
+                    def _():
+                        up_copy(ku, j).wait_recv()
+                        own[ku, core, side, j] += from_low[ku, j]
+
+                    up_copy(ku, j).start()
+
+        kd = it - 2 - (deep - 1 - place)
+
+        @pl.when((kd >= 0) & (kd < ROUNDS))
+        def _():
+            for j in range(deep - 1):
+
+                @pl.when(j < place)
+                def _():
+                    @pl.when(place < deep - 1)
+                    def _():
+                        down_copy(kd, j).wait_recv()
+                        own[kd, core, side, j] += from_high[kd, j]
+
+                    down_copy(kd, j).start()
+
+        kf = it - 1 - deep
+
+        @pl.when((kf >= 0) & (kf < ROUNDS))
+        def _():
+            @pl.when(place > 0)
+            def _():
+                up_copy(kf, place).wait_recv()
+                own[kf, core, side, place] += from_low[kf, place]
+
+            @pl.when(place < deep - 1)
+            def _():
+                down_copy(kf, place).wait_recv()
+                own[kf, core, side, place] += from_high[kf, place]
+
+            out[kf] = own[kf, core, side, place]
+
+        return carry
+
+    lax.fori_loop(0, ROUNDS + deep + 1, phase, 0)
+
+    def drain(k, carry):
+        core_copy(k).wait_send()
+        side_copy(k).wait_send()
+        for j in range(deep):
+
+            @pl.when(j > place)
+            def _():
+                up_copy(k, j).wait_send()
+
+            @pl.when(j < place)
+            def _():
+                down_copy(k, j).wait_send()
+
+        return carry
+
+    lax.fori_loop(0, ROUNDS, drain, 0)
+
+
+def fused(smatrix, amplitude, aberration, beam_list, positions, anchors, masks):
+    width = masks.shape[1]
+    detectors = masks.shape[0]
+    beams = smatrix.shape[3]
+    size = lax.axis_size("beam")
+    per_device = positions.shape[1] // size
+    deep = size // 4
+    spots = positions.reshape(-1, 2)
+    phase_index = jnp.remainder(
+        spots[:, 0:1] * beam_list[None, :, 0] + spots[:, 1:2] * beam_list[None, :, 1], width
+    )
+    theta = aberration[None, :] - 2.0 * math.pi / width * phase_index.astype(jnp.float32)
+    coef = jnp.stack([jnp.cos(theta), jnp.sin(theta)], 0) * amplitude[None, None, :]
+    coef = coef.astype(jnp.bfloat16).reshape(2, TILES, deep, 2, 2, per_device, beams)
+    coef = coef.transpose(0, 4, 3, 2, 1, 5, 6)[..., None, :]
+    same = jnp.eye(TILES, dtype=jnp.bfloat16).reshape(1, 1, 1, 1, TILES, 1, TILES, 1)
+    coef = (coef * same).reshape(2 * TILES * positions.shape[1], TILES * beams)
+    rows = smatrix.shape[0]
+    tail = 2 * (rows - width)
+    keep = jnp.arange(tail)[None, :] // 2 >= anchors[:, 1:2]
+    fold = jnp.stack([keep, ~keep], 1)[..., None].astype(jnp.bfloat16)
+    fold = jnp.broadcast_to(fold, (TILES, 2, tail, beams))
+    table = jnp.asarray(column_table(width))
+    chunk = width // ROUNDS
+    unit = (chunk, 2, 8, width)
+    vmem = pl.BlockSpec(memory_space=pltpu.VMEM)
+    dma = pltpu.SemaphoreType.DMA
+    owned = pl.pallas_call(
+        functools.partial(reduce_kernel, deep, width),
+        out_shape=jax.ShapeDtypeStruct((ROUNDS,) + unit, jnp.float32),
+        in_specs=[pl.BlockSpec(memory_space=pltpu.SMEM)] + [vmem] * 5,
+        out_specs=vmem,
+        scratch_shapes=[
+            pltpu.VMEM((ROUNDS, 2, 2, deep) + unit, jnp.float32),
+            pltpu.VMEM((ROUNDS, 2, deep) + unit, jnp.float32),
+            pltpu.VMEM((ROUNDS, deep) + unit, jnp.float32),
+            pltpu.VMEM((ROUNDS, deep) + unit, jnp.float32),
+            pltpu.VMEM((ROUNDS, deep) + unit, jnp.float32),
+            dma((ROUNDS,)), dma((ROUNDS,)), dma((ROUNDS,)), dma((ROUNDS,)),
+            dma((ROUNDS, deep)), dma((ROUNDS, deep)), dma((ROUNDS, deep)), dma((ROUNDS, deep)),
+        ],
+        compiler_params=pltpu.CompilerParams(
+            collective_id=0, has_side_effects=True, vmem_limit_bytes=60 * 2**20
+        ),
+    )(
+        anchors,
+        smatrix.reshape(rows, 2 * smatrix.shape[1], beams),
+        coef,
+        fold,
+        amplitude.reshape(1, beams),
+        table,
+    )
+    owned = owned.reshape(width, 2, 8, width)
+    norm = owned[0, 0, 0, width // 2]
+    cosine, sine = (jnp.asarray(part, jnp.float32) for part in fourier(width))
+    high = lax.Precision.HIGHEST
+    rotate = jnp.concatenate([cosine, sine], 0)
+    real = jnp.einsum("kr,rul->kul", rotate, owned[:, 0], precision=high)
+    imag = jnp.einsum("kr,rul->kul", rotate, owned[:, 1], precision=high)
+    full_re = real[:width] + imag[width:]
+    full_im = imag[:width] - real[width:]
+    power = full_re * full_re + full_im * full_im
+    signals = jnp.einsum("kul,dkl->ud", power, masks.astype(jnp.float32), precision=high)
+    signals = signals / (norm * width * width)
+    return signals.reshape(TILES, per_device, detectors)
+
+
 def solution(mesh):
     placed = (P(None, None, "parts", "beam"), P("beam"), P("beam"), P("beam", None), P(), P(), P())
-    return jax.shard_map(
-        local, mesh=mesh, in_specs=placed, out_specs=P("parts", "beam", None), check_vma=False
-    )
+
+    def run(smatrix, amplitude, aberration, beam_list, positions, anchors, masks):
+        size = mesh.shape["beam"]
+        rows = TILES * positions.shape[1] // size
+        inner = fused if size % 4 == 0 and rows == 8 else local
+        return jax.shard_map(
+            inner, mesh=mesh, in_specs=placed, out_specs=P("parts", "beam", None), check_vma=False
+        )(smatrix, amplitude, aberration, beam_list, positions, anchors, masks)
+
+    return run

time: 406 us -> 142 us (0.35)
  waiting for transfers between devices: 262 us -> 0 us
  Pallas kernels: 0 us -> 127 us
  local copies, waits for them, and re-layouts: 51.3 us -> 7.27 us
  blocking collectives: 37.3 us -> 0 us
  matrix products: 29 us -> 3.49 us
  between operations: 22.3 us -> 0.75 us
    unnamed x2 -> x0, waiting for transfers between devices: 262 us -> none
    pallas_call x0 -> x1, Pallas kernels: none -> 127 us  [fused(): pl.pallas_call(functools.partial(reduce_kernel, deep, width), out_shape=j...]
    psum x1 -> x0, blocking collectives: 37.3 us -> none  [local(): norm = lax.psum(jnp.sum(amplitude * amplitude), 'beam')]
    reshape x2, local copies, waits for them, and re-layouts: 28.2 us -> 0.77 us  [the longest x1 0.69 us: fused(): return signals.reshape(TILES, per_device, detectors)]
    dot_general x20 -> x3, matrix products: 29 us -> 3.49 us  [the longest x1 1.4 us: fused(): jnp.einsum('kul,dkl->ud', power, masks.astype(jnp.float32), precision=high)]
    dynamic_slice x1 -> x0, local copies, waits for them, and re-layouts: 15.2 us -> none  [window_of(): lax.dynamic_slice(smatrix, (corner[0], corner[1], zero, zero), (width, wi...]
  transfers between devices with their start and end apart: 1 -> 0, of which waited for: 1 -> 0; matrix products, arithmetic and copies ran while one was open for 0% -> 0% of each run, Pallas kernels for 0% -> 0%
where the time goes in v1:
time: 142 us
  Pallas kernels  127 us (89%)
  local copies, waits for them, and re-layouts  7.27 us (5%)
  matrix products  3.49 us (2%)
  other arithmetic  3.33 us (2%)
    pallas_call x1, Pallas kernels, fused(): pl.pallas_call(functools.partial(reduce_kernel, deep, width), out_shape=j...  127 us

profile of v1, /device:TPU:0, one launch (start us, length us, event | category | flops | bytes accessed | tf_op | source)
XLA Modules:
  0.0 141.9 jit_solution(17973458076350355896)
XLA Ops:
  0.0 0.0 copy-start
  0.0 0.9 slice_reduce_fusion
  0.9 0.1 fusion.16
  1.0 0.8 slice_bitcast_fusion.1
  1.8 0.7 copy.18
  2.4 0.1 reshape.398
  2.6 0.1 mul.118
  2.7 0.1 mul.123
  2.8 0.7 broadcast_in_dim.2.fold
  3.5 1.3 fusion.15
  4.8 0.7 fusion.13
  5.5 0.2 broadcast_multiply_fusion
  5.7 0.7 copy.39
  6.3 1.0 convert_element_type.42
  7.3 127.1 %shard_map.100 = f32[8,16,2,8,128]{4,3,2,1,0:T(8,128)} custom-call(s32[2,2]{1,0:T(2,128)} %anchors.1, bf16[144,288,128]{2,1,0:T(8,128)(2,1)} %bitcast.31, bf16[256,256]{1,0:T(8,128)(2,1)} %bitcast.34, bf16[2,2,32,128]{3,2,1,0:T(8,128)(2,1)} %broadcast_in_dim.2.fold, f32[1,128]{1,0:T(1,128)} %bitcast.36, bf16[2,256,256]{2,1,0:T(8,128)(2,1)} %constant.42.clone.table), custom_call_target="tpu_custom_call" | custom-call | tf_op jit(solution)/shard_map/pallas_call | solution.py:346
  134.4 1.3 slice.57
  136.3 1.3 fusion.17
  137.6 0.0 copy-done
  137.6 1.0 fusion.4
  138.7 1.0 fusion.5
  139.7 0.1 fusion.2
  139.8 1.4 fusion
  141.2 0.7 copy.26
  (6 shorter events, 0.1 us)
Async XLA Ops:
  0.0 137.6 %copy-start = (f32[256,128,1]{1,0,2:T(8,128)S(1)}, f32[256,128,1]{1,0,2:T(8,128)}, u32[]{:S(2)}) copy-start(f32[256,128,1]{1,0,2:T(8,128)} %constant.46) | copy-start | bytes 393220

commit v2 on v1

--- a/solution.py
+++ b/solution.py
@@ -10,7 +10,10 @@
 from jax.sharding import PartitionSpec as P
 
 TILES = 2
-ROUNDS = 8
+ROUNDS = 16
+ALONG = 2
+LAG = 3
+HOP = 2
 ROWS = 2
 MESH = pl.DeviceIdType.MESH
 
@@ -133,7 +136,7 @@
 
 def reduce_kernel(
     deep, width, anchors, matrix, coef, fold, power_in, table, out,
-    own, from_core, from_y, from_low, from_high,
+    own, from_core, from_y, from_low, from_high, pair_low, pair_high,
     send_c, recv_c, send_y, recv_y, send_r, recv_r, send_l, recv_l,
 ):
     me = lax.axis_index("beam")
@@ -187,6 +190,27 @@
         return copy(
             own.at[k, core, side, j], from_high.at[k, j], send_l.at[k, j], recv_l.at[k, j], below
         )
+
+    def up_pair(k, j):
+        return copy(
+            own.at[k, core, :, j], pair_low.at[k // 2, j], send_r.at[k, j], recv_r.at[k, j], above
+        )
+
+    def down_pair(k, j):
+        return copy(
+            own.at[k, core, :, j], pair_high.at[k // 2, j], send_l.at[k, j], recv_l.at[k, j], below
+        )
+
+    def last_copy(k):
+        return copy(
+            own.at[k, core, 1 - side, place], from_y.at[k, 0], send_y.at[k], recv_y.at[k], other_side
+        )
+
+    def along(k):
+        return (k < 2 * ALONG) & (lax.rem(k, 2) == 1)
+
+    def across(k):
+        return (k >= 0) & (k < ROUNDS) & jnp.logical_not(along(k))
 
     def window_row(i, tile):
         row = i + jnp.where(i < anchors[tile, 0], width, 0)
@@ -238,78 +262,140 @@
         def _():
             core_copy(k1).wait_recv()
             own[k1, core, 1 - side] += from_core[k1, 1 - side]
-            side_copy(k1).start()
+
+            @pl.when(across(k1))
+            def _():
+                side_copy(k1).start()
+
             own[k1, core, side] += from_core[k1, side]
 
-        k2 = it - 2
-
-        @pl.when((k2 >= 0) & (k2 < ROUNDS))
+        def up_step(k, copy_of, held, index):
+            for j in range(deep - 1, 0, -1):
+
+                @pl.when(j > place)
+                def _():
+                    @pl.when(place > 0)
+                    def _():
+                        copy_of(k, j).wait_recv()
+                        own[(k, core) + index + (j,)] += held(k, j)
+
+                    copy_of(k, j).start()
+
+        def down_step(k, copy_of, held, index):
+            for j in range(deep - 1):
+
+                @pl.when(j < place)
+                def _():
+                    @pl.when(place < deep - 1)
+                    def _():
+                        copy_of(k, j).wait_recv()
+                        own[(k, core) + index + (j,)] += held(k, j)
+
+                    copy_of(k, j).start()
+
+        def finish(k, up_of, down_of, low, high, index):
+            @pl.when(place > 0)
+            def _():
+                up_of(k, place).wait_recv()
+                own[(k, core) + index + (place,)] += low(k, place)
+
+            @pl.when(place < deep - 1)
+            def _():
+                down_of(k, place).wait_recv()
+                own[(k, core) + index + (place,)] += high(k, place)
+
+        def low_pair(k, j):
+            return pair_low[k // 2, j]
+
+        def high_pair(k, j):
+            return pair_high[k // 2, j]
+
+        def low_one(k, j):
+            return from_low[k, j]
+
+        def high_one(k, j):
+            return from_high[k, j]
+
+        both = (slice(None),)
+        ku = it - 1 - HOP * place
+
+        @pl.when((ku >= 0) & along(ku))
+        def _():
+            up_step(ku, up_pair, low_pair, both)
+
+        kd = it - 1 - HOP * (deep - 1 - place)
+
+        @pl.when((kd >= 0) & along(kd))
+        def _():
+            down_step(kd, down_pair, high_pair, both)
+
+        kf = it - 1 - HOP * (deep - 1)
+
+        @pl.when((kf >= 0) & along(kf))
+        def _():
+            finish(kf, up_pair, down_pair, low_pair, high_pair, both)
+            last_copy(kf).start()
+
+        k2 = it - LAG
+
+        @pl.when(across(k2))
         def _():
             side_copy(k2).wait_recv()
             own[k2, core, side] += from_y[k2]
 
-        ku = it - 2 - place
-
-        @pl.when((ku >= 0) & (ku < ROUNDS))
-        def _():
-            for j in range(deep - 1, 0, -1):
-
-                @pl.when(j > place)
-                def _():
-                    @pl.when(place > 0)
-                    def _():
-                        up_copy(ku, j).wait_recv()
-                        own[ku, core, side, j] += from_low[ku, j]
-
-                    up_copy(ku, j).start()
-
-        kd = it - 2 - (deep - 1 - place)
-
-        @pl.when((kd >= 0) & (kd < ROUNDS))
-        def _():
-            for j in range(deep - 1):
-
-                @pl.when(j < place)
-                def _():
-                    @pl.when(place < deep - 1)
-                    def _():
-                        down_copy(kd, j).wait_recv()
-                        own[kd, core, side, j] += from_high[kd, j]
-
-                    down_copy(kd, j).start()
-
-        kf = it - 1 - deep
-
-        @pl.when((kf >= 0) & (kf < ROUNDS))
-        def _():
-            @pl.when(place > 0)
-            def _():
-                up_copy(kf, place).wait_recv()
-                own[kf, core, side, place] += from_low[kf, place]
-
-            @pl.when(place < deep - 1)
-            def _():
-                down_copy(kf, place).wait_recv()
-                own[kf, core, side, place] += from_high[kf, place]
-
-            out[kf] = own[kf, core, side, place]
+        one = (side,)
+        kv = it - LAG - HOP * place
+
+        @pl.when(across(kv))
+        def _():
+            up_step(kv, up_copy, low_one, one)
+
+        ke = it - LAG - HOP * (deep - 1 - place)
+
+        @pl.when(across(ke))
+        def _():
+            down_step(ke, down_copy, high_one, one)
+
+        kg = it - LAG - HOP * (deep - 1)
+
+        @pl.when(across(kg))
+        def _():
+            finish(kg, up_copy, down_copy, low_one, high_one, one)
+            out[kg] = own[kg, core, side, place]
 
         return carry
 
-    lax.fori_loop(0, ROUNDS + deep + 1, phase, 0)
+    lax.fori_loop(0, ROUNDS + LAG + HOP * (deep - 1), phase, 0)
 
     def drain(k, carry):
         core_copy(k).wait_send()
-        side_copy(k).wait_send()
-        for j in range(deep):
-
-            @pl.when(j > place)
-            def _():
-                up_copy(k, j).wait_send()
-
-            @pl.when(j < place)
-            def _():
-                down_copy(k, j).wait_send()
+
+        @pl.when(along(k))
+        def _():
+            last_copy(k).wait()
+            out[k] = own[k, core, side, place] + from_y[k, 0]
+            for j in range(deep):
+
+                @pl.when(j > place)
+                def _():
+                    up_pair(k, j).wait_send()
+
+                @pl.when(j < place)
+                def _():
+                    down_pair(k, j).wait_send()
+
+        @pl.when(across(k))
+        def _():
+            side_copy(k).wait_send()
+            for j in range(deep):
+
+                @pl.when(j > place)
+                def _():
+                    up_copy(k, j).wait_send()
+
+                @pl.when(j < place)
+                def _():
+                    down_copy(k, j).wait_send()
 
         return carry
 
@@ -354,6 +440,8 @@
             pltpu.VMEM((ROUNDS, deep) + unit, jnp.float32),
             pltpu.VMEM((ROUNDS, deep) + unit, jnp.float32),
             pltpu.VMEM((ROUNDS, deep) + unit, jnp.float32),
+            pltpu.VMEM((ALONG, deep, 2) + unit, jnp.float32),
+            pltpu.VMEM((ALONG, deep, 2) + unit, jnp.float32),
             dma((ROUNDS,)), dma((ROUNDS,)), dma((ROUNDS,)), dma((ROUNDS,)),
             dma((ROUNDS, deep)), dma((ROUNDS, deep)), dma((ROUNDS, deep)), dma((ROUNDS, deep)),
         ],

time: 142 us -> 130 us (0.915)
  Pallas kernels: 127 us -> 114 us
    pallas_call x1, Pallas kernels: 127 us -> 114 us  [fused(): pl.pallas_call(functools.partial(reduce_kernel, deep, width), out_shape=j...]
where the time goes in v2:
time: 130 us; the launch traced here: 129 us
  Pallas kernels  114 us (88%)
  local copies, waits for them, and re-layouts  7.27 us (6%)
  matrix products  3.48 us (3%)
  other arithmetic  3.33 us (3%)
    pallas_call x1, Pallas kernels, fused(): pl.pallas_call(functools.partial(reduce_kernel, deep, width), out_shape=j...  114 us

profile of v2, /device:TPU:0, one launch (start us, length us, event | category | flops | bytes accessed | tf_op | source)
XLA Modules:
  0.0 129.2 jit_solution(9582483731471963524)
XLA Ops:
  0.0 0.0 copy-start
  0.0 0.9 slice_reduce_fusion
  0.9 0.1 fusion.16
  1.0 0.8 slice_bitcast_fusion.1
  1.8 0.7 copy.18
  2.4 0.1 reshape.398
  2.6 0.1 mul.118
  2.7 0.1 mul.123
  2.8 0.7 broadcast_in_dim.2.fold
  3.5 1.3 fusion.15
  4.8 0.7 fusion.13
  5.5 0.2 broadcast_multiply_fusion
  5.7 0.7 copy.39
  6.3 1.0 convert_element_type.42
  7.3 114.4 %shard_map.100 = f32[16,8,2,8,128]{4,3,2,1,0:T(8,128)} custom-call(s32[2,2]{1,0:T(2,128)} %anchors.1, bf16[144,288,128]{2,1,0:T(8,128)(2,1)} %bitcast.31, bf16[256,256]{1,0:T(8,128)(2,1)} %bitcast.34, bf16[2,2,32,128]{3,2,1,0:T(8,128)(2,1)} %broadcast_in_dim.2.fold, f32[1,128]{1,0:T(1,128)} %bitcast.36, bf16[2,256,256]{2,1,0:T(8,128)(2,1)} %constant.42.clone.table), custom_call_target="tpu_custom_call" | custom-call | tf_op jit(solution)/shard_map/pallas_call | solution.py:432
  121.7 1.3 slice.57
  123.7 1.3 fusion.17
  124.9 0.0 copy-done
  124.9 1.0 fusion.4
  126.0 1.0 fusion.5
  127.0 0.1 fusion.2
  127.2 1.4 %fusion = f32[8,4]{0,1:T(4,128)S(1)} fusion(f32[128,8,128]{2,0,1:T(8,128)S(1)} %fusion.2, f32[4,128,128]{2,1,0:T(8,128)S(1)} %convert_element_type.42, f32[]{:T(128)} %bitcast.10), kind=kOutput, calls=%fused_computation.1 | convolution fusion | flops 6291488 | bytes 786564 | tf_op jit(solution)/shard_map/kul,dkl->ud/dot_general | solution.py:469
  128.6 0.7 copy.26
  (6 shorter events, 0.1 us)
Async XLA Ops:
  0.0 124.9 %copy-start = (f32[256,128,1]{1,0,2:T(8,128)S(1)}, f32[256,128,1]{1,0,2:T(8,128)}, u32[]{:S(2)}) copy-start(f32[256,128,1]{1,0,2:T(8,128)} %constant.46) | copy-start | bytes 393220
